TPU v7x, 32 devices: a whole 2x2x4 slice. The times are simulated.
32 devices in a mesh: dp: 8 (over z, x), seq: 4 (over y, core).
Axes of the slice: x: 2, y: 2, z: 4, core: 2. Of those that a mesh axis runs over, the one named last changes fastest.
Arguments:
- hidden_states: bfloat16 [8, 512, 4096], P('dp', 'seq'), may hold values from -6 to 6
- queries: bfloat16 [8, 512, 4096], P('dp', 'seq'), may hold values from -20 to 20
- key_states: bfloat16 [8, 512, 512], P('dp', 'seq'), may hold values from -6 to 6
- context_grad: bfloat16 [8, 512, 4096], P('dp', 'seq'), may hold values from -6 to 6
- doc_lengths: int32 [8, 16], P('dp'), may hold values from 1 to 64, 512 in all within a row
- value_weight: bfloat16 [4096, 512], P('dp'), may hold values from -0.09375 to 0.09375
Outputs:
- hidden_grad: bfloat16 [8, 512, 4096], P('dp', 'seq')
- query_grad: bfloat16 [8, 512, 4096], P('dp', 'seq')
- key_grad: bfloat16 [8, 512, 512], P('dp', 'seq')
- value_weight_grad: float32 [4096, 512], P(('dp', 'seq'))
Inputs may be any that keep to these rules, and one draw needn't show every extreme that they name: `doc_lengths`: row s holds the lengths of the 16 documents of sequence s in order; they sum to 512.
All inputs are finite; a program needn't handle non-finite values.
Results may differ from a plain program's by a relative error of at most 0.011.
Values may be sent and summed in bfloat16 or wider, within the bound.
A program may use at most 128 MiB of HBM per device.

v0:
```python
import jax
import jax.numpy as jnp
from jax import lax
from jax.sharding import PartitionSpec as P

HD = 128


far_negative = -1e30


def segment_ids(lengths_row, length):
    doc_ends = jnp.cumsum(lengths_row)
    positions = jnp.arange(length, dtype=jnp.int32)
    return jnp.sum((positions[:, None] >= doc_ends[None, :]).astype(jnp.int32), axis=1)


def attend(query_all, key_all, value_all, grad_all, segment):
    length, head_count, head_width = query_all.shape
    row_block = min(length, max(512, length // 8))
    longest_doc = length // 8
    score_scale = head_width ** (-0.5)
    positions = jnp.arange(length, dtype=jnp.int32)
    key_acc = jnp.zeros((length, head_count, head_width), jnp.float32)
    value_acc = jnp.zeros((length, head_count, head_width), jnp.float32)
    query_parts = []
    for row_start in range(0, length, row_block):
        row_end = row_start + row_block
        key_start = max(0, row_start - longest_doc)
        query_rows = query_all[row_start:row_end]
        grad_rows = grad_all[row_start:row_end]
        key_rows = key_all[key_start:row_end]
        value_rows = value_all[key_start:row_end]
        allowed = (positions[None, key_start:row_end] <= positions[row_start:row_end, None]) & (
            segment[None, key_start:row_end] == segment[row_start:row_end, None]
        )
        scores = (
            jnp.einsum("ihd,jhd->hij", query_rows, key_rows, preferred_element_type=jnp.float32)
            * score_scale
        )
        scores = jnp.where(allowed[None], scores, far_negative)
        row_peak = jnp.max(scores, axis=-1, keepdims=True)
        exponent = jnp.exp(scores - row_peak)
        softmax_weights = exponent / jnp.sum(exponent, axis=-1, keepdims=True)
        weights_low = softmax_weights.astype(jnp.bfloat16)
        attended = jnp.einsum(
            "hij,jhd->ihd", weights_low, value_rows, preferred_element_type=jnp.float32
        )
        row_delta = jnp.sum(grad_rows.astype(jnp.float32) * attended, axis=-1)
        softmax_grad = jnp.einsum(
            "ihd,jhd->hij", grad_rows, value_rows, preferred_element_type=jnp.float32
        )
        score_grad = softmax_weights * (softmax_grad - jnp.transpose(row_delta)[:, :, None])
        score_low = score_grad.astype(jnp.bfloat16)
        query_parts.append(
            (
                jnp.einsum("hij,jhd->ihd", score_low, key_rows, preferred_element_type=jnp.float32)
                * score_scale
            ).astype(jnp.bfloat16)
        )
        key_acc = key_acc.at[key_start:row_end].add(
            jnp.einsum("hij,ihd->jhd", score_low, query_rows, preferred_element_type=jnp.float32)
            * score_scale
        )
        value_acc = value_acc.at[key_start:row_end].add(
            jnp.einsum("hij,ihd->jhd", weights_low, grad_rows, preferred_element_type=jnp.float32)
        )
    return (jnp.concatenate(query_parts, axis=0), key_acc, value_acc)


def body(hidden_states, queries, key_states, context_grad, doc_lengths, value_weight):
    tokens = hidden_states.shape[1]
    rows_here = hidden_states[0]
    heads_total = queries.shape[2] // HD
    kv_heads = key_states.shape[2] // HD
    group_size = heads_total // kv_heads
    columns = rows_here
    values = jnp.dot(
        columns,
        lax.all_gather(value_weight, "dp", axis=0, tiled=True),
        preferred_element_type=jnp.float32,
    ).astype(jnp.bfloat16)
    query_heads = queries[0].reshape(tokens, heads_total, HD)
    grad_heads = context_grad[0].reshape(tokens, heads_total, HD)
    query_all, grad_all = (
        lax.all_to_all(query_heads, "seq", split_axis=1, concat_axis=0, tiled=True),
        lax.all_to_all(grad_heads, "seq", split_axis=1, concat_axis=0, tiled=True),
    )
    length = query_all.shape[0]
    key_three = key_states[0].reshape(tokens, kv_heads, HD)
    value_three = values.reshape(tokens, kv_heads, HD)
    segment = segment_ids(doc_lengths[0], length)
    key_all, value_all = (
        lax.all_to_all(
            jnp.repeat(key_three, group_size, axis=1),
            "seq",
            split_axis=1,
            concat_axis=0,
            tiled=True,
        ),
        lax.all_to_all(
            jnp.repeat(value_three, group_size, axis=1),
            "seq",
            split_axis=1,
            concat_axis=0,
            tiled=True,
        ),
    )
    query_back, key_back, value_back = attend(query_all, key_all, value_all, grad_all, segment)
    key_home, value_home = (
        lax.all_to_all(
            key_back.astype(jnp.bfloat16), "seq", split_axis=0, concat_axis=1, tiled=True
        ).astype(key_back.dtype),
        lax.all_to_all(
            value_back.astype(jnp.bfloat16), "seq", split_axis=0, concat_axis=1, tiled=True
        ).astype(value_back.dtype),
    )
    key_sum = jnp.sum(key_home.reshape(tokens, kv_heads, group_size, HD), axis=2)
    value_sum = jnp.sum(value_home.reshape(tokens, kv_heads, group_size, HD), axis=2)
    query_home = lax.all_to_all(query_back, "seq", split_axis=0, concat_axis=1, tiled=True)
    value_low = value_sum.reshape(tokens, kv_heads * HD).astype(jnp.bfloat16)
    hidden_grad = jnp.einsum(
        "tc,rc->tr",
        value_low,
        lax.all_gather(value_weight, "dp", axis=0, tiled=True),
        preferred_element_type=jnp.float32,
    )
    columns = rows_here
    weight_grad = lax.psum_scatter(
        jnp.einsum("tr,tc->rc", columns, value_low, preferred_element_type=jnp.float32),
        ("dp", "seq"),
        scatter_dimension=0,
        tiled=True,
    )
    return (
        hidden_grad.astype(jnp.bfloat16)[None],
        query_home.reshape(tokens, heads_total * HD)[None],
        key_sum.reshape(tokens, kv_heads * HD).astype(jnp.bfloat16)[None],
        weight_grad,
    )


def solution(mesh):
    return jax.shard_map(
        body,
        mesh=mesh,
        in_specs=(
            P("dp", "seq", None),
            P("dp", "seq", None),
            P("dp", "seq", None),
            P("dp", "seq", None),
            P("dp", None),
            P("dp", None),
        ),
        out_specs=(
            P("dp", "seq", None),
            P("dp", "seq", None),
            P("dp", "seq", None),
            P(("dp", "seq"), None),
        ),
        check_vma=False,
    )
```

profile of v0, /device:TPU:0, one launch (start us, length us, event | category | flops | bytes accessed | tf_op | source)
XLA Modules:
  0.0 270.5 jit_solution(17113018626907057216)
XLA Ops:
  8.0 0.0 copy-start
  8.0 0.0 copy-start.6
  8.0 0.0 all-gather.2.cloned.1.call-start
  8.1 0.7 all-gather.2.cloned.1.call-update
  8.8 1.6 copy.93
  10.4 1.3 copy.94
  11.7 4.2 %all-to-all-start = ((bf16[128,32,128]{2,0,1:T(8,128)(2,1)}), bf16[128,32,128]{2,0,1:T(8,128)(2,1)S(1)}, u32[]{:S(2)}, u32[]{:S(2)}) async-start(bf16[128,32,128]{2,0,1:T(8,128)(2,1)} %copy.94), calls=%async_computation | async-start | bytes 2097152 | tf_op jit(solution)/shard_map/all_to_all | solution.py:86
  15.9 0.0 copy-done.6
  16.0 14.4 %all-to-all-done = bf16[128,32,128]{2,0,1:T(8,128)(2,1)S(1)} async-done(((bf16[128,32,128]{2,0,1:T(8,128)(2,1)}), bf16[128,32,128]{2,0,1:T(8,128)(2,1)S(1)}, u32[]{:S(2)}, u32[]{:S(2)}) %all-to-all-start) | async-done | bytes 1048608 | tf_op jit(solution)/shard_map/all_to_all | solution.py:86
  30.4 1.2 broadcast_in_dim.19
  31.6 3.7 %all-to-all-start.1 = ((bf16[128,32,128]{2,0,1:T(8,128)(2,1)}), bf16[128,32,128]{2,0,1:T(8,128)(2,1)S(1)}, u32[]{:S(2)}, u32[]{:S(2)}) async-start(bf16[128,32,128]{2,0,1:T(8,128)(2,1)} %bitcast.84), calls=%async_computation.1 | async-start | bytes 2097152 | tf_op jit(solution)/shard_map/all_to_all | solution.py:94
  35.3 2.3 copy.100
  37.5 2.3 copy.101
  39.8 9.9 %all-to-all-done.1 = bf16[128,32,128]{2,0,1:T(8,128)(2,1)S(1)} async-done(((bf16[128,32,128]{2,0,1:T(8,128)(2,1)}), bf16[128,32,128]{2,0,1:T(8,128)(2,1)S(1)}, u32[]{:S(2)}, u32[]{:S(2)}) %all-to-all-start.1) | async-done | bytes 1048608 | tf_op jit(solution)/shard_map/all_to_all | solution.py:94
  49.7 4.2 %all-to-all-start.2 = ((bf16[128,32,128]{2,0,1:T(8,128)(2,1)}), bf16[128,32,128]{2,0,1:T(8,128)(2,1)}, u32[]{:S(2)}, u32[]{:S(2)}) async-start(bf16[128,32,128]{2,0,1:T(8,128)(2,1)} %copy.101), calls=%async_computation.2 | async-start | bytes 2097152 | tf_op jit(solution)/shard_map/all_to_all | solution.py:87
  53.9 0.0 reduce-scatter.2.cloned.1.call-start
  54.0 0.0 copy-done.7
  54.0 0.1 copy.92
  54.1 0.1 reduce.10
  54.2 0.1 convert_reduce_fusion
  54.3 0.2 fusion.15
  54.6 1.0 copy.96
  55.6 1.0 copy.99
  56.6 11.8 %all-to-all-done.2 = bf16[128,32,128]{2,0,1:T(8,128)(2,1)} async-done(((bf16[128,32,128]{2,0,1:T(8,128)(2,1)}), bf16[128,32,128]{2,0,1:T(8,128)(2,1)}, u32[]{:S(2)}, u32[]{:S(2)}) %all-to-all-start.2) | async-done | bytes 1048608 | tf_op jit(solution)/shard_map/all_to_all | solution.py:87
  68.5 1.3 copy.103
  69.8 0.0 copy-done.3
  69.8 7.5 %fusion.20 = (f32[8,512]{1,0:T(8,128)S(1)}, f32[8,512,512]{1,2,0:T(8,128)}) fusion(pred[512,512]{0,1:T(8,128)(4,1)S(1)} %fusion.15, bf16[512,8,128]{2,0,1:T(8,128)(2,1)S(1)} %bitcast.96, bf16[512,8,128]{2,0,1:T(8,128)(2,1)} %bitcast.98), kind=kOutput, calls=%fused_computation.34 | convolution fusion | flops 545260032 | bytes 10764288 | tf_op jit(solution)/shard_map/sub | solution.py:43
  77.3 4.6 %fusion.7 = bf16[8,512,512]{1,2,0:T(8,128)(2,1)S(1)} fusion(f32[8,512,512]{1,2,0:T(8,128)} %get-tuple-element.69, f32[8,512]{1,0:T(8,128)S(1)} %get-tuple-element.68), kind=kLoop, calls=%fused_computation.13 | loop fusion | flops 4194304 | bytes 12599296 | tf_op jit(solution)/shard_map/convert_element_type | solution.py:45
  81.9 0.0 copy-start.1
  81.9 1.3 fusion.9
  83.2 0.7 copy.104
  83.9 16.9 %all_to_all.105 = bf16[512,8,128]{2,1,0:T(8,128)(2,1)S(1)} all-to-all(bf16[512,8,128]{2,1,0:T(8,128)(2,1)S(1)} %copy.104), channel_id=1, replica_groups=mesh['dp'=8,'seq'=4] {'seq'}, dimensions={0} | all-to-all | bytes 2097152 | tf_op jit(solution)/shard_map/all_to_all | solution.py:114
  100.8 0.7 reduce.9
  101.5 0.1 copy.105
  101.6 0.0 copy-done
  101.6 4.5 %convolution_bitcast_fusion = f32[4096,512]{0,1:T(8,128)} fusion(bf16[128,512]{0,1:T(8,128)(2,1)S(1)} %bitcast.94, bf16[1,128,4096]{2,1,0:T(8,128)(2,1)S(1)} %copy-done), kind=kOutput, calls=%fused_computation.5 | convolution fusion | flops 536870912 | bytes 9568256 | tf_op jit(solution)/shard_map/tr,tc->rc/dot_general | solution.py:130
  106.1 0.0 reduce-scatter.2.cloned.1.call-update
  106.1 0.0 all-gather.2.cloned.1.call-done
  106.1 0.0 copy-start.2
  106.2 3.1 %fusion.12 = bf16[16,4,8,128]{3,2,1,0:T(8,128)(2,1)S(1)} fusion(bf16[4096,512]{1,0:T(8,128)(2,1)} %all-gather.2.cloned.1.call-done, bf16[1,128,4096]{2,1,0:T(8,128)(2,1)S(1)} %copy-done), kind=kOutput, calls=%fused_computation.23 | convolution fusion | flops 536936448 | bytes 5373952 | tf_op jit(solution)/shard_map/dot_general | solution.py:78
  109.2 0.2 broadcast_in_dim.36
  109.5 28.8 %all_to_all.106 = bf16[128,32,128]{2,0,1:T(8,128)(2,1)S(1)} all-to-all(bf16[128,32,128]{2,0,1:T(8,128)(2,1)S(1)} %bitcast.85), channel_id=1, replica_groups=mesh['dp'=8,'seq'=4] {'seq'}, dimensions={1} | all-to-all | bytes 2097152 | tf_op jit(solution)/shard_map/all_to_all | solution.py:101
  138.3 0.1 copy.108
  138.4 1.8 fusion.8
  140.2 0.0 copy-start.5
  140.2 4.8 %fusion.1 = bf16[8,512,512]{1,2,0:T(8,128)(2,1)S(1)} fusion(f32[8,512]{1,0:T(8,128)S(1)} %bitcast.104, f32[8,512,512]{1,2,0:T(8,128)} %get-tuple-element.69, f32[8,512]{1,0:T(8,128)S(1)} %get-tuple-element.68, bf16[512,8,128]{2,0,1:T(8,128)(2,1)S(1)} %bitcast.93, bf16[512,8,128]{2,0,1:T(8,128)(2,1)S(1)} %bitcast.91), kind=kOutput, calls=%fused_computation.2 | convolution fusion | flops 545259520 | bytes 14712832 | tf_op jit(solution)/shard_map/ihd,jhd->hij/dot_general | solution.py:50
  145.0 0.0 copy-start.4
  145.0 1.5 fusion.10
  146.5 0.4 copy-done.8
  147.0 1.6 copy.113
  148.6 3.5 %all-to-all-start.5 = ((bf16[512,8,128]{2,1,0:T(8,128)(2,1)}), bf16[512,8,128]{2,1,0:T(8,128)(2,1)S(1)}, u32[]{:S(2)}, u32[]{:S(2)}) async-start(bf16[512,8,128]{2,1,0:T(8,128)(2,1)} %copy.113), calls=%async_computation.5 | async-start | bytes 2097152 | tf_op jit(solution)/shard_map/all_to_all | solution.py:120
  152.1 3.5 %fusion.11 = bf16[512,8,128]{2,0,1:T(8,128)(2,1)S(1)} fusion(bf16[8,512,512]{1,2,0:T(8,128)(2,1)} %copy-done.8, bf16[512,8,128]{2,0,1:T(8,128)(2,1)S(1)} %bitcast.97), kind=kOutput, calls=%fused_computation.21 | convolution fusion | flops 537919488 | bytes 6291456 | tf_op jit(solution)/shard_map/hij,ihd->jhd/dot_general | solution.py:62
  155.6 1.7 copy.115
  157.4 21.1 %all-to-all-done.5 = bf16[512,8,128]{2,1,0:T(8,128)(2,1)S(1)} async-done(((bf16[512,8,128]{2,1,0:T(8,128)(2,1)}), bf16[512,8,128]{2,1,0:T(8,128)(2,1)S(1)}, u32[]{:S(2)}, u32[]{:S(2)}) %all-to-all-start.5) | async-done | bytes 1048608 | tf_op jit(solution)/shard_map/all_to_all | solution.py:120
  178.4 3.5 %all-to-all-start.6 = ((bf16[512,8,128]{2,1,0:T(8,128)(2,1)}), bf16[512,8,128]{2,1,0:T(8,128)(2,1)S(1)}, u32[]{:S(2)}, u32[]{:S(2)}) async-start(bf16[512,8,128]{2,1,0:T(8,128)(2,1)} %copy.115), calls=%async_computation.6 | async-start | bytes 2097152 | tf_op jit(solution)/shard_map/all_to_all | solution.py:111
  181.9 4.7 %fusion.3 = bf16[1,128,4096]{2,1,0:T(8,128)(2,1)} fusion(bf16[128,512]{0,1:T(8,128)(2,1)S(1)} %bitcast.95, bf16[4096,512]{1,0:T(8,128)(2,1)} %all-gather.2.cloned.1.call-done), kind=kOutput, calls=%fused_computation.8 | convolution fusion | flops 537395200 | bytes 5373952 | tf_op jit(solution)/shard_map/tc,rc->tr/dot_general | solution.py:122
  186.7 1.2 copy.114
  187.8 2.3 broadcast_in_dim_reshape.3
  190.1 18.4 %all-to-all-done.6 = bf16[512,8,128]{2,1,0:T(8,128)(2,1)S(1)} async-done(((bf16[512,8,128]{2,1,0:T(8,128)(2,1)}), bf16[512,8,128]{2,1,0:T(8,128)(2,1)S(1)}, u32[]{:S(2)}, u32[]{:S(2)}) %all-to-all-start.6) | async-done | bytes 1048608 | tf_op jit(solution)/shard_map/all_to_all | solution.py:111
  208.5 0.7 reduce_sum.52
  209.2 0.1 copy.116
  209.3 0.8 copy.117
  210.1 51.2 %reduce-scatter.2.cloned.1.call-done = f32[128,512]{0,1:T(8,128)} async-done(((f32[4096,512]{0,1:T(8,128)}), f32[128,512]{0,1:T(8,128)}) %reduce-scatter.2.cloned.1.call-update) | async-done | bytes 262160 | tf_op jit(solution)/shard_map/reduce_scatter | solution.py:129
  261.3 1.8 copy.118
  (11 shorter events, 0.1 us)
Async XLA Ops:
  8.0 93.6 %copy-start = (bf16[1,128,4096]{2,1,0:T(8,128)(2,1)S(1)}, bf16[1,128,4096]{2,1,0:T(8,128)(2,1)}, u32[]{:S(2)}) copy-start(bf16[1,128,4096]{2,1,0:T(8,128)(2,1)} %param.14) | copy-start | bytes 3145732
  8.0 7.9 %copy-start.6 = (bf16[1,128,512]{2,1,0:T(8,128)(2,1)S(1)}, bf16[1,128,512]{2,1,0:T(8,128)(2,1)}, u32[]{:S(2)}) copy-start(bf16[1,128,512]{2,1,0:T(8,128)(2,1)} %param.16) | copy-start | bytes 393220
  8.0 98.1 %all-gather.2.cloned.1.call-start = ((), (), s32[]{:S(2)}) async-start(), calls=%async_computation.8 | async-start | bytes 4718592 | tf_op jit(solution)/shard_map/all_gather | solution.py:125
  11.7 18.7 %all-to-all-start = ((bf16[128,32,128]{2,0,1:T(8,128)(2,1)}), bf16[128,32,128]{2,0,1:T(8,128)(2,1)S(1)}, u32[]{:S(2)}, u32[]{:S(2)}) async-start(bf16[128,32,128]{2,0,1:T(8,128)(2,1)} %copy.94), calls=%async_computation | async-start | bytes 2097152 | tf_op jit(solution)/shard_map/all_to_all | solution.py:86
  31.6 22.4 %copy-start.7 = (s32[1,16]{1,0:T(1,128)S(1)}, s32[1,16]{1,0:T(1,128)}, u32[]{:S(2)}) copy-start(s32[1,16]{1,0:T(1,128)} %param.18) | copy-start | bytes 196
  31.6 18.1 %all-to-all-start.1 = ((bf16[128,32,128]{2,0,1:T(8,128)(2,1)}), bf16[128,32,128]{2,0,1:T(8,128)(2,1)S(1)}, u32[]{:S(2)}, u32[]{:S(2)}) async-start(bf16[128,32,128]{2,0,1:T(8,128)(2,1)} %bitcast.84), calls=%async_computation.1 | async-start | bytes 2097152 | tf_op jit(solution)/shard_map/all_to_all | solution.py:94
  49.7 18.8 %all-to-all-start.2 = ((bf16[128,32,128]{2,0,1:T(8,128)(2,1)}), bf16[128,32,128]{2,0,1:T(8,128)(2,1)}, u32[]{:S(2)}, u32[]{:S(2)}) async-start(bf16[128,32,128]{2,0,1:T(8,128)(2,1)} %copy.101), calls=%async_computation.2 | async-start | bytes 2097152 | tf_op jit(solution)/shard_map/all_to_all | solution.py:87
  53.9 207.4 %reduce-scatter.2.cloned.1.call-start = ((), (), s32[]{:S(2)}) async-start(), calls=%async_computation.9 | async-start | bytes 8650752 | tf_op jit(solution)/shard_map/reduce_scatter | solution.py:129
  55.6 14.2 %copy-start.3 = (bf16[4,128,8,128]{3,1,0,2:T(8,128)(2,1)S(1)}, bf16[4,128,8,128]{3,1,0,2:T(8,128)(2,1)}, u32[]{:S(2)}) copy-start(bf16[4,128,8,128]{3,1,0,2:T(8,128)(2,1)} %copy.96) | copy-start | bytes 3145732
  81.9 2.0 copy-start.1
  106.1 32.2 %copy-start.2 = (bf16[8,512,512]{1,2,0:T(8,128)(2,1)S(1)}, bf16[8,512,512]{1,2,0:T(8,128)(2,1)}, u32[]{:S(2)}) copy-start(bf16[8,512,512]{1,2,0:T(8,128)(2,1)} %copy-done.1) | copy-start | bytes 12582916
  140.2 4.8 %copy-start.5 = (bf16[4,128,8,128]{3,1,0,2:T(8,128)(2,1)S(1)}, bf16[4,128,8,128]{3,1,0,2:T(8,128)(2,1)}, u32[]{:S(2)}) copy-start(bf16[4,128,8,128]{3,1,0,2:T(8,128)(2,1)} %copy.99) | copy-start | bytes 3145732
  145.0 2.0 copy-start.8
  145.0 7.1 %copy-start.4 = (bf16[4,128,8,128]{3,1,0,2:T(8,128)(2,1)S(1)}, bf16[4,128,8,128]{3,1,0,2:T(8,128)(2,1)}, u32[]{:S(2)}) copy-start(bf16[4,128,8,128]{3,1,0,2:T(8,128)(2,1)} %copy.96) | copy-start | bytes 3145732
  148.6 29.8 %all-to-all-start.5 = ((bf16[512,8,128]{2,1,0:T(8,128)(2,1)}), bf16[512,8,128]{2,1,0:T(8,128)(2,1)S(1)}, u32[]{:S(2)}, u32[]{:S(2)}) async-start(bf16[512,8,128]{2,1,0:T(8,128)(2,1)} %copy.113), calls=%async_computation.5 | async-start | bytes 2097152 | tf_op jit(solution)/shard_map/all_to_all | solution.py:120
  178.4 30.1 %all-to-all-start.6 = ((bf16[512,8,128]{2,1,0:T(8,128)(2,1)}), bf16[512,8,128]{2,1,0:T(8,128)(2,1)S(1)}, u32[]{:S(2)}, u32[]{:S(2)}) async-start(bf16[512,8,128]{2,1,0:T(8,128)(2,1)} %copy.115), calls=%async_computation.6 | async-start | bytes 2097152 | tf_op jit(solution)/shard_map/all_to_all | solution.py:111
Sparse Core Ops, SparseCore 0:
  11.0 76.0 all-gather.1
Sparse Core Ops, SparseCore 1:
  106.2 155.1 reduce-scatter.1
where the time goes:
time: 271 us
  waiting for transfers between devices  127 us (47%)
  blocking collectives  45.7 us (17%)
  matrix products  32.6 us (12%)
  local copies, waits for them, and re-layouts  23.3 us (9%)
  starting transfers between devices  19.2 us (7%)
  between operations  15.8 us (6%)
  other arithmetic  6.44 us (2%)
    reduce_scatter x1, waiting for transfers between devices, body(): lax.psum_scatter(jnp.einsum('tr,tc->rc', columns, value_low, preferred_el...  51.2 us
    all_to_all x1, blocking collectives, body(): lax.all_to_all(jnp.repeat(value_three, group_size, axis=1), 'seq', split_...  28.8 us
    all_to_all x1, waiting for transfers between devices, body(): lax.all_to_all(query_back, 'seq', split_axis=0, concat_axis=1, tiled=True)  21.1 us
    all_to_all x1, waiting for transfers between devices, body(): lax.all_to_all(key_back.astype(jnp.bfloat16), 'seq', split_axis=0, concat...  18.4 us
    all_to_all x1, blocking collectives, body(): lax.all_to_all(value_back.astype(jnp.bfloat16), 'seq', split_axis=0, conc...  16.9 us
    all_to_all x1, waiting for transfers between devices, body(): lax.all_to_all(query_heads, 'seq', split_axis=1, concat_axis=0, tiled=True)  14.4 us
    all_to_all x1, waiting for transfers between devices, body(): lax.all_to_all(grad_heads, 'seq', split_axis=1, concat_axis=0, tiled=True)  11.8 us
    all_to_all x1, waiting for transfers between devices, body(): lax.all_to_all(jnp.repeat(key_three, group_size, axis=1), 'seq', split_ax...  9.88 us
  transfers between devices with their start and end apart: 7, of which 6 were waited for; matrix products, arithmetic and copies ran while one was open for 22% of the time, Pallas kernels for 0%

commit v1 on v0

v1 whole, which is shorter than its diff:
```python
import functools

import jax
import jax.numpy as jnp
from jax import lax
from jax.experimental import pallas as pl
from jax.experimental.pallas import tpu as pltpu
from jax.sharding import PartitionSpec as P

HD = 128
FAR_NEGATIVE = -1e30
MESH = pl.DeviceIdType.MESH
BF16 = jnp.bfloat16
F32 = jnp.float32


def dot(a, b, ca, cb):
    return lax.dot_general(a, b, (((ca,), (cb,)), ((), ())), preferred_element_type=F32)


def kernel(
    sizes,
    hidden_ref,
    query_ref,
    key_ref,
    grad_ref,
    lengths_ref,
    weight_ref,
    hidden_grad_ref,
    query_grad_ref,
    key_grad_ref,
    weight_grad_ref,
    hs,
    hq,
    wq,
    kf,
    pv,
    pr,
    vf,
    ws,
    ka,
    kh,
    kr,
    vc,
    va,
    vl,
    gp,
    gs,
    xr,
    zs,
    zr,
    hg,
    hr,
    s_hid, r_hid, s_wz, s_wx, r_w, s_k, r_k, s_pv, r_pv, s_kg, r_kg,
    s_vc, r_vc, s_gx, r_gx, s_gz, r_gz, s_hg, r_hg,
):
    T, n_seq, n_dp, na, nb, halo, R, kv, group = sizes
    C = kv * HD
    Kw = halo + T
    L = n_seq * T
    scale = HD ** -0.5
    W = n_dp * R
    s = lax.axis_index("seq")
    d = lax.axis_index("dp")
    a, b = lax.div(d, nb), lax.rem(d, nb)
    seq_peers = [lax.rem(s + o, n_seq) for o in range(1, n_seq)]
    seq_from = [lax.rem(s + n_seq - o, n_seq) for o in range(1, n_seq)]
    a_peers = [lax.rem(a + o, na) for o in range(1, na)]
    a_from = [lax.rem(a + na - o, na) for o in range(1, na)]
    b_peers = [lax.rem(b + o, nb) for o in range(1, nb)]
    b_from = [lax.rem(b + nb - o, nb) for o in range(1, nb)]

    sends = []

    def rows(i, n):
        return pl.ds(pl.multiple_of(i * n, n), n)

    def copy(src, dst, ss, rs, where):
        return pltpu.make_async_remote_copy(
            src_ref=src, dst_ref=dst, send_sem=ss, recv_sem=rs, device_id=where, device_id_type=MESH
        )

    def start(*args):
        c = copy(*args)
        c.start()
        sends.append(c)

    barrier = pltpu.get_barrier_semaphore()
    for p in seq_peers:
        pl.semaphore_signal(barrier, inc=1, device_id={"seq": p}, device_id_type=MESH)
    for p in a_peers:
        pl.semaphore_signal(barrier, inc=1, device_id={"dp": p * nb + b}, device_id_type=MESH)
    for p in b_peers:
        pl.semaphore_signal(barrier, inc=1, device_id={"dp": a * nb + p}, device_id_type=MESH)

    kf[halo:, :] = key_ref[...]
    wq[rows(d, R), :] = weight_ref[rows(s, R), :]
    for t in range(n_seq):
        if R % 128 == 0:
            for e in range(n_dp):
                at = (e * n_seq + t) * R
                hs[t, :, e * R : (e + 1) * R] = hidden_ref[:, at : at + R]
        else:
            hs[t] = hidden_ref[t]

    pl.semaphore_wait(barrier, n_seq - 1 + na - 1 + nb - 1)

    def w_slot(i):
        return wq.at[rows(i, R), :]

    for o, p in enumerate(a_peers):
        start(w_slot(d), w_slot(d), s_wz.at[o], r_w.at[d], {"dp": p * nb + b})

    def pass_on(i, k):
        for o, p in enumerate(b_peers):
            start(w_slot(i), w_slot(i), s_wx.at[k, o], r_w.at[i], {"dp": a * nb + p})

    pass_on(d, 0)

    blocks = []
    left = halo
    while left > 0:
        m = min(T, left)
        blocks.append((left - m, m))
        left -= m
    for o, (at, m) in enumerate(blocks):
        start(
            key_ref.at[T - m :, :], kf.at[at : at + m, :], s_k.at[o], r_k.at[o],
            {"seq": lax.rem(s + o + 1, n_seq)},
        )
    for o, p in enumerate(seq_peers):
        start(hs.at[p], hq.at[rows(s, T), :], s_hid.at[o], r_hid.at[s], {"seq": p})
    hq[rows(s, T), :] = hs[s]

    query_at = s * T + lax.broadcasted_iota(jnp.int32, (Kw, T), 1)
    key_at = s * T - halo + lax.broadcasted_iota(jnp.int32, (Kw, T), 0)
    begin = jnp.zeros((Kw, T), jnp.int32)
    end = jnp.int32(0)
    for i in range(lengths_ref.shape[1]):
        end = end + lengths_ref[0, i]
        begin = jnp.where(query_at >= end, end, begin)
    seen = (key_at >= begin) & (key_at <= query_at)
    bias = jnp.where(seen, 0.0, FAR_NEGATIVE).astype(F32)

    for o, (at, m) in enumerate(blocks):
        copy(
            key_ref.at[T - m :, :], kf.at[at : at + m, :], s_k.at[o], r_k.at[o],
            {"seq": lax.rem(s + o + 1, n_seq)},
        ).wait_recv()

    def stack(ref, g):
        return jnp.concatenate(
            [ref[:, pl.ds(pl.multiple_of((g * group + h) * HD, HD), HD)] for h in range(group)], axis=0
        )

    def head(g):
        return pl.ds(pl.multiple_of(g * HD, HD), HD)

    def scores(g, _):
        qs = stack(query_ref, g)
        sc = dot(kf[:, head(g)], qs, 1, 1) * scale + jnp.concatenate([bias] * group, axis=1)
        e = jnp.exp(sc - jnp.max(sc, axis=0, keepdims=True))
        ws[g] = e / jnp.sum(e, axis=0, keepdims=True)
        return 0

    lax.fori_loop(0, kv, scores, 0)

    for k, p in enumerate(a_from):
        i = p * nb + b
        copy(w_slot(i), w_slot(i), s_wz.at[k], r_w.at[i], {"dp": d}).wait_recv()
        pass_on(i, k + 1)
    for o, p in enumerate(seq_from):
        copy(hs.at[p], hq.at[rows(p, T), :], s_hid.at[o], r_hid.at[p], {"seq": s}).wait_recv()
    for p in b_from:
        for z in range(na):
            i = z * nb + p
            copy(w_slot(i), w_slot(i), s_wz.at[0], r_w.at[i], {"dp": d}).wait_recv()

    pv[:halo, :] = jnp.zeros((halo, C), BF16)

    def project(t, _):
        pv[pl.ds(pl.multiple_of(halo + t * T, 16), T), :] = dot(hq[rows(t, T), :], wq[...], 1, 0).astype(BF16)
        return 0

    lax.fori_loop(0, n_seq, project, 0)

    def pv_rows(t):
        return pv.at[pl.ds(pl.multiple_of(t * T, T), Kw), :]

    for o, p in enumerate(seq_peers):
        start(pv_rows(p), pr.at[s], s_pv.at[o], r_pv.at[s], {"seq": p})
    pr[s] = pv[pl.ds(pl.multiple_of(s * T, T), Kw), :]
    for o, p in enumerate(seq_from):
        copy(pv_rows(p), pr.at[p], s_pv.at[o], r_pv.at[p], {"seq": s}).wait_recv()
    total = pr[0].astype(F32)
    for t in range(1, n_seq):
        total = total + pr[t].astype(F32)
    vf[...] = total.astype(BF16)

    def grads(g, _):
        qs = stack(query_ref, g)
        cs = stack(grad_ref, g)
        kg = kf[:, head(g)]
        w = ws[g]
        wl = w.astype(BF16)
        sg = dot(vf[:, head(g)], cs, 1, 1)
        delta = jnp.sum(wl.astype(F32) * sg, axis=0, keepdims=True)
        ds = (w * (sg - delta)).astype(BF16)
        vc[s, :, head(g)] = dot(wl, cs, 1, 0).astype(BF16)
        ka[:, head(g)] = dot(ds, qs, 1, 0) * scale
        qg = (dot(ds, kg, 0, 0) * scale).astype(BF16)
        for h in range(group):
            query_grad_ref[:, pl.ds(pl.multiple_of((g * group + h) * HD, HD), HD)] = qg[h * T : (h + 1) * T]
        return 0

    lax.fori_loop(0, kv, grads, 0)

    for o, p in enumerate(seq_peers):
        start(vc.at[s], vc.at[s], s_vc.at[o], r_vc.at[s], {"seq": p})
    kh[...] = ka[:halo, :].astype(BF16)
    for o, (at, m) in enumerate(blocks):
        start(
            kh.at[at : at + m, :], kr.at[at : at + m, :], s_kg.at[o], r_kg.at[o],
            {"seq": lax.rem(s + 2 * n_seq - o - 1, n_seq)},
        )
    va[...] = jnp.zeros((halo + L, C), F32)
    for o, p in enumerate(seq_from):
        copy(vc.at[p], vc.at[p], s_vc.at[o], r_vc.at[p], {"seq": s}).wait_recv()
    for t in range(n_seq):
        va[t * T : t * T + Kw, :] += vc[t].astype(F32)
    vl[...] = va[halo:, :].astype(BF16)

    part = min(W, 256)
    for c in range(0, W, part):
        x = dot(hq[:, c : c + part], vl[...], 0, 0)
        gp[c : c + part, :] = x
        gs[c : c + part, :] = x.astype(BF16)
    for k, z in enumerate(a_peers + [a]):
        for o, p in enumerate(b_peers):
            start(
                gs.at[rows(z * nb + p, R), :], xr.at[b, rows(z, R), :], s_gx.at[k, o], r_gx.at[b, z],
                {"dp": a * nb + p},
            )

    for o, p in enumerate(seq_peers + [s]):
        x = dot(vl[rows(p, T), :], wq[...], 1, 1).astype(BF16)
        if o < n_seq - 1:
            hg[p] = x
            start(hg.at[p], hr.at[s], s_hg.at[o], r_hg.at[s], {"seq": p})
        else:
            hr[s] = x

    def reduced(z):
        x = gp[rows(z * nb + b, R), :]
        for p in b_from:
            copy(
                gs.at[rows(z * nb + p, R), :], xr.at[p, rows(z, R), :], s_gx.at[0, 0], r_gx.at[p, z],
                {"dp": d},
            ).wait_recv()
            x = x + xr[p, rows(z, R), :].astype(F32)
        return x

    for o, z in enumerate(a_peers):
        zs[z] = reduced(z).astype(BF16)
        start(zs.at[z], zr.at[a], s_gz.at[o], r_gz.at[a], {"dp": z * nb + b})
    mine = reduced(a)

    for o, (at, m) in enumerate(blocks):
        copy(
            kh.at[at : at + m, :], kr.at[at : at + m, :], s_kg.at[o], r_kg.at[o], {"seq": s}
        ).wait_recv()
        ka[Kw - m :, :] += kr[at : at + m, :].astype(F32)
    key_grad_ref[...] = ka[halo:, :].astype(BF16)

    for o, p in enumerate(a_from):
        copy(zs.at[p], zr.at[p], s_gz.at[o], r_gz.at[p], {"dp": d}).wait_recv()
        mine = mine + zr[p].astype(F32)
    weight_grad_ref[...] = mine

    for o, p in enumerate(seq_from):
        copy(hg.at[p], hr.at[p], s_hg.at[o], r_hg.at[p], {"seq": s}).wait_recv()
    for t in range(n_seq):
        if R % 128 == 0:
            for e in range(n_dp):
                at = (e * n_seq + t) * R
                hidden_grad_ref[:, at : at + R] = hr[t, :, e * R : (e + 1) * R]
        else:
            hidden_grad_ref[t] = hr[t]
    for c in sends:
        c.wait_send()


def body(n_dp, n_seq, hidden_states, queries, key_states, context_grad, doc_lengths, value_weight):
    _, T, D = hidden_states.shape
    C = key_states.shape[2]
    kv = C // HD
    group = queries.shape[2] // C
    L = T * n_seq
    halo = min(L, L // 8)
    R = value_weight.shape[0] // n_seq
    na = 4 if n_dp % 4 == 0 else n_dp
    nb = n_dp // na
    W = n_dp * R
    Kw = halo + T
    n_halo = -(-halo // T)
    sizes = (T, n_seq, n_dp, na, nb, halo, R, kv, group)
    hidden = hidden_states[0]
    wide = R % 128 == 0
    if not wide:
        hidden = hidden.reshape(T, n_dp, n_seq, R).transpose(2, 0, 1, 3).reshape(n_seq, T, W)
    vmem = pl.BlockSpec(memory_space=pltpu.VMEM)
    sem = lambda *shape: pltpu.SemaphoreType.DMA(shape)
    out = pl.pallas_call(
        functools.partial(kernel, sizes),
        out_shape=(
            jax.ShapeDtypeStruct(hidden.shape, BF16),
            jax.ShapeDtypeStruct((T, queries.shape[2]), BF16),
            jax.ShapeDtypeStruct((T, C), BF16),
            jax.ShapeDtypeStruct((R, C), F32),
        ),
        in_specs=[vmem, vmem, vmem, vmem, pl.BlockSpec(memory_space=pltpu.SMEM), vmem],
        out_specs=(vmem,) * 4,
        scratch_shapes=[
            pltpu.VMEM((n_seq, T, W), BF16),
            pltpu.VMEM((L, W), BF16),
            pltpu.VMEM((W, C), BF16),
            pltpu.VMEM((Kw, C), BF16),
            pltpu.VMEM((halo + L, C), BF16),
            pltpu.VMEM((n_seq, Kw, C), BF16),
            pltpu.VMEM((Kw, C), BF16),
            pltpu.VMEM((kv, Kw, group * T), F32),
            pltpu.VMEM((Kw, C), F32),
            pltpu.VMEM((halo, C), BF16),
            pltpu.VMEM((halo, C), BF16),
            pltpu.VMEM((n_seq, Kw, C), BF16),
            pltpu.VMEM((halo + L, C), F32),
            pltpu.VMEM((L, C), BF16),
            pltpu.VMEM((W, C), F32),
            pltpu.VMEM((W, C), BF16),
            pltpu.VMEM((nb, na * R, C), BF16),
            pltpu.VMEM((na, R, C), BF16),
            pltpu.VMEM((na, R, C), BF16),
            pltpu.VMEM((n_seq, T, W), BF16),
            pltpu.VMEM((n_seq, T, W), BF16),
            sem(n_seq), sem(n_seq),
            sem(na), sem(na, nb), sem(n_dp),
            sem(n_halo), sem(n_halo),
            sem(n_seq), sem(n_seq),
            sem(n_halo), sem(n_halo),
            sem(n_seq), sem(n_seq),
            sem(na, nb), sem(nb, na),
            sem(na), sem(na),
            sem(n_seq), sem(n_seq),
        ],
        compiler_params=pltpu.CompilerParams(
            collective_id=0, has_side_effects=True, vmem_limit_bytes=56 * 1024 * 1024
        ),
        name="attention_backward",
    )(hidden, queries[0], key_states[0], context_grad[0], doc_lengths, value_weight)
    hidden_grad = out[0]
    if not wide:
        hidden_grad = hidden_grad.reshape(n_seq, T, n_dp, R).transpose(1, 2, 0, 3).reshape(T, D)
    return hidden_grad[None], out[1][None], out[2][None], out[3]


def solution(mesh):
    return jax.shard_map(
        functools.partial(body, mesh.shape["dp"], mesh.shape["seq"]),
        mesh=mesh,
        in_specs=(
            P("dp", "seq", None),
            P("dp", "seq", None),
            P("dp", "seq", None),
            P("dp", "seq", None),
            P("dp", None),
            P("dp", None),
        ),
        out_specs=(
            P("dp", "seq", None),
            P("dp", "seq", None),
            P("dp", "seq", None),
            P(("dp", "seq"), None),
        ),
        check_vma=False,
    )
```

time: 271 us -> 69.4 us (0.26)
  the two profiles are of different devices: /device:TPU:0 before, /device:TPU:11 now
where the time goes in v1:
time: 69.4 us; the launch traced here: 68.5 us
  Pallas kernels  62.7 us (90%)
  local copies, waits for them, and re-layouts  5.1 us (7%)
    pallas_call x1, Pallas kernels, body(): pl.pallas_call(functools.partial(kernel, sizes), out_shape=(jax.ShapeDtyp...  62.7 us
    unnamed x10, local copies, waits for them, and re-layouts  5.1 us

profile of v1, /device:TPU:11, one launch (start us, length us, event | category | flops | bytes accessed | tf_op | source)
XLA Modules:
  0.0 68.5 jit_solution(7416657949156910831)
XLA Ops:
  0.6 62.7 %attention_backward.1 = (bf16[128,4096]{1,0:T(8,128)(2,1)}, bf16[128,4096]{1,0:T(8,128)(2,1)}, bf16[128,512]{1,0:T(8,128)(2,1)}, f32[128,512]{1,0:T(8,128)}) custom-call(bf16[128,4096]{1,0:T(8,128)(2,1)} %bitcast.9, bf16[128,4096]{1,0:T(8,128)(2,1)} %bitcast.10, bf16[128,512]{1,0:T(8,128)(2,1)} %bitcast.12, bf16[128,4096]{1,0:T(8,128)(2,1)} %bitcast.11, ...), custom_call_target="tpu_custom_call" | custom-call | tf_op jit(solution)/shard_map/attention_backward/pallas_call | solution.py:313
  63.4 0.0 copy-start
  63.4 2.4 %copy.14 = bf16[1,128,4096]{2,1,0:T(8,128)(2,1)} copy(bf16[1,128,4096]{2,1,0:T(8,128)(2,1)} %bitcast.8) | data formatting | bytes 2097152
  65.8 0.0 copy-done
  65.8 0.0 copy-start.2
  65.8 1.0 %copy.15 = bf16[1,128,4096]{2,1,0:T(8,128)(2,1)} copy(bf16[1,128,4096]{2,1,0:T(8,128)(2,1)S(1)} %bitcast.7) | data formatting | bytes 2097152
  66.7 0.1 copy-done.2
  66.8 0.0 copy-start.1
  66.8 0.7 copy.16
  67.5 0.3 copy-done.1
  67.8 0.7 %copy.17 = f32[128,512]{1,0:T(8,128)} copy(f32[128,512]{1,0:T(8,128)S(1)} %copy-done.1) | data formatting | bytes 524288
Async XLA Ops:
  63.4 2.4 %copy-start = (bf16[128,4096]{1,0:T(8,128)(2,1)S(1)}, bf16[128,4096]{1,0:T(8,128)(2,1)}, u32[]{:S(2)}) copy-start(bf16[128,4096]{1,0:T(8,128)(2,1)} %get-tuple-element.9) | copy-start | bytes 3145732
  65.8 1.0 %copy-start.2 = (bf16[128,512]{1,0:T(8,128)(2,1)S(1)}, bf16[128,512]{1,0:T(8,128)(2,1)}, u32[]{:S(2)}) copy-start(bf16[128,512]{1,0:T(8,128)(2,1)} %get-tuple-element.10) | copy-start | bytes 393220
  66.8 1.0 %copy-start.1 = (f32[128,512]{1,0:T(8,128)S(1)}, f32[128,512]{1,0:T(8,128)}, u32[]{:S(2)}) copy-start(f32[128,512]{1,0:T(8,128)} %get-tuple-element.19) | copy-start | bytes 786436

commit v2 on v1

--- a/solution.py
+++ b/solution.py
@@ -20,21 +20,27 @@
 
 def kernel(
     sizes,
-    hidden_ref,
-    query_ref,
+    hidden_any,
+    query_any,
     key_ref,
-    grad_ref,
+    grad_any,
     lengths_ref,
     weight_ref,
     hidden_grad_ref,
-    query_grad_ref,
+    query_grad_any,
     key_grad_ref,
     weight_grad_ref,
+    hid,
+    query_ref,
+    grad_ref,
+    query_grad_ref,
     hs,
     hq,
     wq,
     kf,
     pv,
+    pc,
+    px,
     pr,
     vf,
     ws,
@@ -51,7 +57,7 @@
     zr,
     hg,
     hr,
-    s_hid, r_hid, s_wz, s_wx, r_w, s_k, r_k, s_pv, r_pv, s_kg, r_kg,
+    s_in, s_hid, r_hid, s_wz, s_wx, r_w, s_k, r_k, s_pc, r_pc, s_pv, r_pv, s_kg, r_kg,
     s_vc, r_vc, s_gx, r_gx, s_gz, r_gz, s_hg, r_hg,
 ):
     T, n_seq, n_dp, na, nb, halo, R, kv, group = sizes
@@ -80,10 +86,31 @@
             src_ref=src, dst_ref=dst, send_sem=ss, recv_sem=rs, device_id=where, device_id_type=MESH
         )
 
-    def start(*args):
-        c = copy(*args)
-        c.start()
-        sends.append(c)
+    def start(*args, cond=None):
+        if cond is None:
+            copy(*args).start()
+        else:
+
+            @pl.when(cond)
+            def _():
+                copy(*args).start()
+
+        sends.append((cond, args))
+
+    def wait_recv(*args, cond=None):
+        if cond is None:
+            copy(*args).wait_recv()
+        else:
+
+            @pl.when(cond)
+            def _():
+                copy(*args).wait_recv()
+
+    y, core = lax.div(s, 2), lax.rem(s, 2)
+    ny = n_seq // 2
+    mate = 1 - core
+    y_peers = [lax.rem(y + o, ny) for o in range(1, ny)]
+    y_from = [lax.rem(y + ny - o, ny) for o in range(1, ny)]
 
     barrier = pltpu.get_barrier_semaphore()
     for p in seq_peers:
@@ -93,29 +120,59 @@
     for p in b_peers:
         pl.semaphore_signal(barrier, inc=1, device_id={"dp": a * nb + p}, device_id_type=MESH)
 
-    kf[halo:, :] = key_ref[...]
-    wq[rows(d, R), :] = weight_ref[rows(s, R), :]
+    inputs = [
+        (hidden_any, hid),
+        (weight_ref.at[rows(s, R), :], wq.at[rows(d, R), :]),
+        (key_ref, kf.at[halo:, :]),
+        (query_any, query_ref),
+        (grad_any, grad_ref),
+    ]
+    inputs = [pltpu.make_async_copy(x, z, s_in.at[i]) for i, (x, z) in enumerate(inputs)]
+    for x in inputs:
+        x.start()
+    inputs[0].wait()
     for t in range(n_seq):
         if R % 128 == 0:
             for e in range(n_dp):
                 at = (e * n_seq + t) * R
-                hs[t, :, e * R : (e + 1) * R] = hidden_ref[:, at : at + R]
+                hs[t, :, e * R : (e + 1) * R] = hid[:, at : at + R]
         else:
-            hs[t] = hidden_ref[t]
+            hs[t] = hid[t]
+    inputs[1].wait()
 
     pl.semaphore_wait(barrier, n_seq - 1 + na - 1 + nb - 1)
 
     def w_slot(i):
         return wq.at[rows(i, R), :]
 
-    for o, p in enumerate(a_peers):
-        start(w_slot(d), w_slot(d), s_wz.at[o], r_w.at[d], {"dp": p * nb + b})
-
-    def pass_on(i, k):
+    ahead = jnp.minimum(a + 1, na - 1) * nb + b
+    behind = jnp.maximum(a - 1, 0) * nb + b
+
+    def pass_on(i, k, cond=None):
         for o, p in enumerate(b_peers):
-            start(w_slot(i), w_slot(i), s_wx.at[k, o], r_w.at[i], {"dp": a * nb + p})
-
+            start(w_slot(i), w_slot(i), s_wx.at[k, o], r_w.at[i], {"dp": a * nb + p}, cond=cond)
+
+    start(w_slot(d), w_slot(d), s_wz.at[0, 0], r_w.at[d], {"dp": ahead}, cond=a < na - 1)
+    start(w_slot(d), w_slot(d), s_wz.at[0, 1], r_w.at[d], {"dp": behind}, cond=a > 0)
     pass_on(d, 0)
+
+    def hop(k):
+        i = jnp.maximum(a - k, 0) * nb + b
+        here = a >= k
+        wait_recv(w_slot(i), w_slot(i), s_wz.at[k, 0], r_w.at[i], {"dp": d}, cond=here)
+        start(
+            w_slot(i), w_slot(i), s_wz.at[k, 0], r_w.at[i], {"dp": ahead},
+            cond=jnp.logical_and(here, a < na - 1),
+        )
+        pass_on(i, 2 * k, here)
+        i = jnp.minimum(a + k, na - 1) * nb + b
+        here = a + k < na
+        wait_recv(w_slot(i), w_slot(i), s_wz.at[k, 1], r_w.at[i], {"dp": d}, cond=here)
+        start(
+            w_slot(i), w_slot(i), s_wz.at[k, 1], r_w.at[i], {"dp": behind},
+            cond=jnp.logical_and(here, a > 0),
+        )
+        pass_on(i, 2 * k + 1, here)
 
     blocks = []
     left = halo
@@ -142,6 +199,8 @@
     seen = (key_at >= begin) & (key_at <= query_at)
     bias = jnp.where(seen, 0.0, FAR_NEGATIVE).astype(F32)
 
+    for x in inputs[2:]:
+        x.wait()
     for o, (at, m) in enumerate(blocks):
         copy(
             key_ref.at[T - m :, :], kf.at[at : at + m, :], s_k.at[o], r_k.at[o],
@@ -163,18 +222,17 @@
         ws[g] = e / jnp.sum(e, axis=0, keepdims=True)
         return 0
 
-    lax.fori_loop(0, kv, scores, 0)
-
-    for k, p in enumerate(a_from):
-        i = p * nb + b
-        copy(w_slot(i), w_slot(i), s_wz.at[k], r_w.at[i], {"dp": d}).wait_recv()
-        pass_on(i, k + 1)
+    for k in range(max(kv, na - 1)):
+        if k < kv:
+            scores(k, 0)
+        if k < na - 1:
+            hop(k + 1)
     for o, p in enumerate(seq_from):
         copy(hs.at[p], hq.at[rows(p, T), :], s_hid.at[o], r_hid.at[p], {"seq": s}).wait_recv()
     for p in b_from:
         for z in range(na):
             i = z * nb + p
-            copy(w_slot(i), w_slot(i), s_wz.at[0], r_w.at[i], {"dp": d}).wait_recv()
+            copy(w_slot(i), w_slot(i), s_wx.at[0, 0], r_w.at[i], {"dp": d}).wait_recv()
 
     pv[:halo, :] = jnp.zeros((halo, C), BF16)
 
@@ -187,14 +245,20 @@
     def pv_rows(t):
         return pv.at[pl.ds(pl.multiple_of(t * T, T), Kw), :]
 
-    for o, p in enumerate(seq_peers):
-        start(pv_rows(p), pr.at[s], s_pv.at[o], r_pv.at[s], {"seq": p})
-    pr[s] = pv[pl.ds(pl.multiple_of(s * T, T), Kw), :]
-    for o, p in enumerate(seq_from):
-        copy(pv_rows(p), pr.at[p], s_pv.at[o], r_pv.at[p], {"seq": s}).wait_recv()
-    total = pr[0].astype(F32)
-    for t in range(1, n_seq):
-        total = total + pr[t].astype(F32)
+    for o, p in enumerate(y_peers + [y]):
+        start(pv_rows(p * 2 + mate), pc.at[p], s_pc.at[o], r_pc.at[p], {"seq": y * 2 + mate})
+
+    def pair(p):
+        copy(pv_rows(p * 2 + core), pc.at[p], s_pc.at[0], r_pc.at[p], {"seq": s}).wait_recv()
+        return pv[pl.ds(pl.multiple_of((p * 2 + core) * T, T), Kw), :].astype(F32) + pc[p].astype(F32)
+
+    for o, p in enumerate(y_peers):
+        px[p] = pair(p).astype(BF16)
+        start(px.at[p], pr.at[y], s_pv.at[o], r_pv.at[y], {"seq": p * 2 + core})
+    total = pair(y)
+    for o, p in enumerate(y_from):
+        copy(px.at[p], pr.at[p], s_pv.at[o], r_pv.at[p], {"seq": s}).wait_recv()
+        total = total + pr[p].astype(F32)
     vf[...] = total.astype(BF16)
 
     def grads(g, _):
@@ -215,8 +279,11 @@
 
     lax.fori_loop(0, kv, grads, 0)
 
-    for o, p in enumerate(seq_peers):
-        start(vc.at[s], vc.at[s], s_vc.at[o], r_vc.at[s], {"seq": p})
+    saved = pltpu.make_async_copy(query_grad_ref, query_grad_any, s_in.at[0])
+    saved.start()
+    for o, p in enumerate(y_peers):
+        start(vc.at[s], vc.at[s], s_vc.at[o], r_vc.at[s], {"seq": p * 2 + core})
+    start(vc.at[s], vc.at[s], s_vc.at[ny - 1], r_vc.at[s], {"seq": y * 2 + mate})
     kh[...] = ka[:halo, :].astype(BF16)
     for o, (at, m) in enumerate(blocks):
         start(
@@ -224,23 +291,35 @@
             {"seq": lax.rem(s + 2 * n_seq - o - 1, n_seq)},
         )
     va[...] = jnp.zeros((halo + L, C), F32)
-    for o, p in enumerate(seq_from):
-        copy(vc.at[p], vc.at[p], s_vc.at[o], r_vc.at[p], {"seq": s}).wait_recv()
+    for o, p in enumerate(y_from):
+        i = p * 2 + core
+        copy(vc.at[i], vc.at[i], s_vc.at[o], r_vc.at[i], {"seq": s}).wait_recv()
+        start(vc.at[i], vc.at[i], s_vc.at[ny + o], r_vc.at[i], {"seq": y * 2 + mate})
+    for p in [y] + y_from:
+        i = p * 2 + mate
+        copy(vc.at[i], vc.at[i], s_vc.at[0], r_vc.at[i], {"seq": s}).wait_recv()
     for t in range(n_seq):
         va[t * T : t * T + Kw, :] += vc[t].astype(F32)
     vl[...] = va[halo:, :].astype(BF16)
 
-    part = min(W, 256)
+    def send_terms(z):
+        for o, p in enumerate(b_peers):
+            start(
+                gs.at[rows(z * nb + p, R), :], xr.at[b, rows(z, R), :], s_gx.at[z, o], r_gx.at[b, z],
+                {"dp": a * nb + p},
+            )
+
+    wide = nb * R % 128 == 0
+    part = nb * R if wide else W
     for c in range(0, W, part):
         x = dot(hq[:, c : c + part], vl[...], 0, 0)
         gp[c : c + part, :] = x
         gs[c : c + part, :] = x.astype(BF16)
-    for k, z in enumerate(a_peers + [a]):
-        for o, p in enumerate(b_peers):
-            start(
-                gs.at[rows(z * nb + p, R), :], xr.at[b, rows(z, R), :], s_gx.at[k, o], r_gx.at[b, z],
-                {"dp": a * nb + p},
-            )
+        if wide:
+            send_terms(c // part)
+    if not wide:
+        for z in range(na):
+            send_terms(z)
 
     for o, p in enumerate(seq_peers + [s]):
         x = dot(vl[rows(p, T), :], wq[...], 1, 1).astype(BF16)
@@ -286,8 +365,32 @@
                 hidden_grad_ref[:, at : at + R] = hr[t, :, e * R : (e + 1) * R]
         else:
             hidden_grad_ref[t] = hr[t]
-    for c in sends:
-        c.wait_send()
+    saved.wait()
+    for cond, args in sends:
+        if cond is None:
+            copy(*args).wait_send()
+        else:
+
+            @pl.when(cond)
+            def _():
+                copy(*args).wait_send()
+
+
+def write(*refs):
+    n = len(refs) // 2
+    sem = refs[-1]
+    copies = []
+    for x, z in zip(refs[:n], refs[n:-1]):
+        many = x.shape[0]
+        step = many // 4 if x.shape[-1] > 1024 and many % 64 == 0 else many
+        for at in range(0, many, step):
+            copies.append(
+                pltpu.make_async_copy(x.at[at : at + step], z.at[at : at + step], sem.at[len(copies)])
+            )
+    for c in copies:
+        c.start()
+    for c in copies:
+        c.wait()
 
 
 def body(n_dp, n_seq, hidden_states, queries, key_states, context_grad, doc_lengths, value_weight):
@@ -309,6 +412,8 @@
     if not wide:
         hidden = hidden.reshape(T, n_dp, n_seq, R).transpose(2, 0, 1, 3).reshape(n_seq, T, W)
     vmem = pl.BlockSpec(memory_space=pltpu.VMEM)
+    hbm = pl.BlockSpec(memory_space=pl.ANY)
+    ny = n_seq // 2
     sem = lambda *shape: pltpu.SemaphoreType.DMA(shape)
     out = pl.pallas_call(
         functools.partial(kernel, sizes),
@@ -318,15 +423,21 @@
             jax.ShapeDtypeStruct((T, C), BF16),
             jax.ShapeDtypeStruct((R, C), F32),
         ),
-        in_specs=[vmem, vmem, vmem, vmem, pl.BlockSpec(memory_space=pltpu.SMEM), vmem],
-        out_specs=(vmem,) * 4,
+        in_specs=[hbm, hbm, hbm, hbm, pl.BlockSpec(memory_space=pltpu.SMEM), hbm],
+        out_specs=(vmem, hbm, vmem, vmem),
         scratch_shapes=[
+            pltpu.VMEM(hidden.shape, BF16),
+            pltpu.VMEM((T, queries.shape[2]), BF16),
+            pltpu.VMEM((T, queries.shape[2]), BF16),
+            pltpu.VMEM((T, queries.shape[2]), BF16),
             pltpu.VMEM((n_seq, T, W), BF16),
             pltpu.VMEM((L, W), BF16),
             pltpu.VMEM((W, C), BF16),
             pltpu.VMEM((Kw, C), BF16),
             pltpu.VMEM((halo + L, C), BF16),
-            pltpu.VMEM((n_seq, Kw, C), BF16),
+            pltpu.VMEM((ny, Kw, C), BF16),
+            pltpu.VMEM((ny, Kw, C), BF16),
+            pltpu.VMEM((ny, Kw, C), BF16),
             pltpu.VMEM((Kw, C), BF16),
             pltpu.VMEM((kv, Kw, group * T), F32),
             pltpu.VMEM((Kw, C), F32),
@@ -342,12 +453,13 @@
             pltpu.VMEM((na, R, C), BF16),
             pltpu.VMEM((n_seq, T, W), BF16),
             pltpu.VMEM((n_seq, T, W), BF16),
-            sem(n_seq), sem(n_seq),
-            sem(na), sem(na, nb), sem(n_dp),
+            sem(5), sem(n_seq), sem(n_seq),
+            sem(na, 2), sem(2 * na, nb), sem(n_dp),
             sem(n_halo), sem(n_halo),
-            sem(n_seq), sem(n_seq),
+            sem(ny), sem(ny),
+            sem(ny), sem(ny),
             sem(n_halo), sem(n_halo),
-            sem(n_seq), sem(n_seq),
+            sem(2 * ny), sem(n_seq),
             sem(na, nb), sem(nb, na),
             sem(na), sem(na),
             sem(n_seq), sem(n_seq),
@@ -357,6 +469,15 @@
         ),
         name="attention_backward",
     )(hidden, queries[0], key_states[0], context_grad[0], doc_lengths, value_weight)
+    if wide:
+        out = pl.pallas_call(
+            write,
+            out_shape=[jax.ShapeDtypeStruct(x.shape, x.dtype) for x in out],
+            in_specs=[hbm] * 4,
+            out_specs=[hbm] * 4,
+            scratch_shapes=[sem(10)],
+            name="write",
+        )(*out)
     hidden_grad = out[0]
     if not wide:
         hidden_grad = hidden_grad.reshape(n_seq, T, n_dp, R).transpose(1, 2, 0, 3).reshape(T, D)

time: 69.4 us -> 140 us (2.02)
  Pallas kernels: 62.7 us -> 138 us
  local copies, waits for them, and re-layouts: 5.1 us -> 0 us
    pallas_call x0 -> x1, Pallas kernels: none -> 76.6 us  [body(): pl.pallas_call(write, out_shape=[jax.ShapeDtypeStruct(x.shape, x.dtype) f...]
    unnamed x10 -> x0, local copies, waits for them, and re-layouts: 5.1 us -> none
    pallas_call x1, Pallas kernels: 62.7 us -> 61 us  [body(): pl.pallas_call(functools.partial(kernel, sizes), out_shape=(jax.ShapeDtyp...]
where the time goes in v2:
time: 140 us; the launch traced here: 138 us
  Pallas kernels  138 us (99%)
    pallas_call x1, Pallas kernels, body(): pl.pallas_call(write, out_shape=[jax.ShapeDtypeStruct(x.shape, x.dtype) f...  76.6 us
    pallas_call x1, Pallas kernels, body(): pl.pallas_call(functools.partial(kernel, sizes), out_shape=(jax.ShapeDtyp...  61 us

profile of v2, /device:TPU:11, one launch (start us, length us, event | category | flops | bytes accessed | tf_op | source)
XLA Modules:
  0.0 138.3 jit_solution(1086064994456895477)
XLA Ops:
  0.6 61.0 %attention_backward.1 = (bf16[128,4096]{1,0:T(8,128)(2,1)}, bf16[128,4096]{1,0:T(8,128)(2,1)}, bf16[128,512]{1,0:T(8,128)(2,1)}, f32[128,512]{1,0:T(8,128)}) custom-call(bf16[128,4096]{1,0:T(8,128)(2,1)} %bitcast.7, bf16[128,4096]{1,0:T(8,128)(2,1)} %bitcast.8, bf16[128,512]{1,0:T(8,128)(2,1)} %bitcast.10, bf16[128,4096]{1,0:T(8,128)(2,1)} %bitcast.9, ...), custom_call_target="tpu_custom_call" | custom-call | tf_op jit(solution)/shard_map/attention_backward/pallas_call | solution.py:418
  61.7 76.6 %write.1 = (bf16[128,4096]{1,0:T(8,128)(2,1)}, bf16[128,4096]{1,0:T(8,128)(2,1)}, bf16[128,512]{1,0:T(8,128)(2,1)}, f32[128,512]{1,0:T(8,128)}) custom-call(bf16[128,4096]{1,0:T(8,128)(2,1)} %get-tuple-element.12.refs_0_, bf16[128,4096]{1,0:T(8,128)(2,1)} %get-tuple-element.13.refs_1_, bf16[128,512]{1,0:T(8,128)(2,1)} %get-tuple-element.14.refs_2_, ...), custom_call_target="tpu_custom_call" | custom-call | tf_op jit(solution)/shard_map/write/pallas_call | solution.py:473

commit v3 on v2

--- a/solution.py
+++ b/solution.py
@@ -302,24 +302,26 @@
         va[t * T : t * T + Kw, :] += vc[t].astype(F32)
     vl[...] = va[halo:, :].astype(BF16)
 
-    def send_terms(z):
+    def send_terms(k, z):
         for o, p in enumerate(b_peers):
             start(
-                gs.at[rows(z * nb + p, R), :], xr.at[b, rows(z, R), :], s_gx.at[z, o], r_gx.at[b, z],
+                gs.at[rows(z * nb + p, R), :], xr.at[b, rows(z, R), :], s_gx.at[k, o], r_gx.at[b, z],
                 {"dp": a * nb + p},
             )
 
-    wide = nb * R % 128 == 0
-    part = nb * R if wide else W
-    for c in range(0, W, part):
-        x = dot(hq[:, c : c + part], vl[...], 0, 0)
-        gp[c : c + part, :] = x
-        gs[c : c + part, :] = x.astype(BF16)
-        if wide:
-            send_terms(c // part)
-    if not wide:
-        for z in range(na):
-            send_terms(z)
+    part = nb * R
+    if part % 128 == 0:
+        for k, z in enumerate(a_peers + [a]):
+            x = dot(hq[:, rows(z, part)], vl[...], 0, 0)
+            gp[rows(z, part), :] = x
+            gs[rows(z, part), :] = x.astype(BF16)
+            send_terms(k, z)
+    else:
+        x = dot(hq[...], vl[...], 0, 0)
+        gp[...] = x
+        gs[...] = x.astype(BF16)
+        for k, z in enumerate(a_peers + [a]):
+            send_terms(k, z)
 
     for o, p in enumerate(seq_peers + [s]):
         x = dot(vl[rows(p, T), :], wq[...], 1, 1).astype(BF16)
@@ -378,19 +380,8 @@
 
 def write(*refs):
     n = len(refs) // 2
-    sem = refs[-1]
-    copies = []
-    for x, z in zip(refs[:n], refs[n:-1]):
-        many = x.shape[0]
-        step = many // 4 if x.shape[-1] > 1024 and many % 64 == 0 else many
-        for at in range(0, many, step):
-            copies.append(
-                pltpu.make_async_copy(x.at[at : at + step], z.at[at : at + step], sem.at[len(copies)])
-            )
-    for c in copies:
-        c.start()
-    for c in copies:
-        c.wait()
+    for x, z in zip(refs[:n], refs[n:]):
+        z[...] = x[...]
 
 
 def body(n_dp, n_seq, hidden_states, queries, key_states, context_grad, doc_lengths, value_weight):
@@ -470,12 +461,13 @@
         name="attention_backward",
     )(hidden, queries[0], key_states[0], context_grad[0], doc_lengths, value_weight)
     if wide:
+        blocks = [pl.BlockSpec((x.shape[0] // 4, x.shape[1]), lambda i: (i, 0)) for x in out]
         out = pl.pallas_call(
             write,
+            grid=(4,),
             out_shape=[jax.ShapeDtypeStruct(x.shape, x.dtype) for x in out],
-            in_specs=[hbm] * 4,
-            out_specs=[hbm] * 4,
-            scratch_shapes=[sem(10)],
+            in_specs=blocks,
+            out_specs=blocks,
             name="write",
         )(*out)
     hidden_grad = out[0]

time: 140 us -> 63.9 us (0.46); the launches traced: 138 us -> 63.7 us
  Pallas kernels: 138 us -> 63.1 us
    pallas_call x1, Pallas kernels: 76.6 us -> 3.84 us  [body(): pl.pallas_call(write, grid=(4,), out_shape=[jax.ShapeDtypeStruct(x.shape,...]
    pallas_call x1, Pallas kernels: 61 us -> 59.2 us  [body(): pl.pallas_call(functools.partial(kernel, sizes), out_shape=(jax.ShapeDtyp...]
where the time goes in v3:
time: 63.9 us; the launch traced here: 63.7 us
  Pallas kernels  63.1 us (99%)
  between operations  0.64 us (1%)
    pallas_call x1, Pallas kernels, body(): pl.pallas_call(functools.partial(kernel, sizes), out_shape=(jax.ShapeDtyp...  59.2 us
    pallas_call x1, Pallas kernels, body(): pl.pallas_call(write, grid=(4,), out_shape=[jax.ShapeDtypeStruct(x.shape,...  3.84 us

profile of v3, /device:TPU:11, one launch (start us, length us, event | category | flops | bytes accessed | tf_op | source)
XLA Modules:
  0.0 63.7 jit_solution(8554497711729165394)
XLA Ops:
  0.6 59.2 %attention_backward.1 = (bf16[128,4096]{1,0:T(8,128)(2,1)}, bf16[128,4096]{1,0:T(8,128)(2,1)}, bf16[128,512]{1,0:T(8,128)(2,1)}, f32[128,512]{1,0:T(8,128)}) custom-call(bf16[128,4096]{1,0:T(8,128)(2,1)} %bitcast.7, bf16[128,4096]{1,0:T(8,128)(2,1)} %bitcast.8, bf16[128,512]{1,0:T(8,128)(2,1)} %bitcast.10, bf16[128,4096]{1,0:T(8,128)(2,1)} %bitcast.9, ...), custom_call_target="tpu_custom_call" | custom-call | tf_op jit(solution)/shard_map/attention_backward/pallas_call | solution.py:409
  59.9 3.8 %write.1 = (bf16[128,4096]{1,0:T(8,128)(2,1)}, bf16[128,4096]{1,0:T(8,128)(2,1)}, bf16[128,512]{1,0:T(8,128)(2,1)}, f32[128,512]{1,0:T(8,128)}) custom-call(bf16[128,4096]{1,0:T(8,128)(2,1)} %get-tuple-element.12.refs_0_, bf16[128,4096]{1,0:T(8,128)(2,1)} %get-tuple-element.13.refs_1_, bf16[128,512]{1,0:T(8,128)(2,1)} %get-tuple-element.14.refs_2_, ...), custom_call_target="tpu_custom_call" | custom-call | tf_op jit(solution)/shard_map/write/pallas_call | solution.py:465

commit v4 on v3

--- a/solution.py
+++ b/solution.py
@@ -73,6 +73,8 @@
     seq_from = [lax.rem(s + n_seq - o, n_seq) for o in range(1, n_seq)]
     a_peers = [lax.rem(a + o, na) for o in range(1, na)]
     a_from = [lax.rem(a + na - o, na) for o in range(1, na)]
+    far = lax.rem(a + 2, na)
+    a_order = [far, far + 1 - 2 * lax.rem(far, 2), a + 1 - 2 * lax.rem(a, 2)] if na == 4 else a_peers
     b_peers = [lax.rem(b + o, nb) for o in range(1, nb)]
     b_from = [lax.rem(b + nb - o, nb) for o in range(1, nb)]
 
@@ -311,7 +313,7 @@
 
     part = nb * R
     if part % 128 == 0:
-        for k, z in enumerate(a_peers + [a]):
+        for k, z in enumerate(a_order + [a]):
             x = dot(hq[:, rows(z, part)], vl[...], 0, 0)
             gp[rows(z, part), :] = x
             gs[rows(z, part), :] = x.astype(BF16)
@@ -320,7 +322,7 @@
         x = dot(hq[...], vl[...], 0, 0)
         gp[...] = x
         gs[...] = x.astype(BF16)
-        for k, z in enumerate(a_peers + [a]):
+        for k, z in enumerate(a_order + [a]):
             send_terms(k, z)
 
     for o, p in enumerate(seq_peers + [s]):
@@ -341,7 +343,7 @@
             x = x + xr[p, rows(z, R), :].astype(F32)
         return x
 
-    for o, z in enumerate(a_peers):
+    for o, z in enumerate(a_order):
         zs[z] = reduced(z).astype(BF16)
         start(zs.at[z], zr.at[a], s_gz.at[o], r_gz.at[a], {"dp": z * nb + b})
     mine = reduced(a)
@@ -461,10 +463,10 @@
         name="attention_backward",
     )(hidden, queries[0], key_states[0], context_grad[0], doc_lengths, value_weight)
     if wide:
-        blocks = [pl.BlockSpec((x.shape[0] // 4, x.shape[1]), lambda i: (i, 0)) for x in out]
+        blocks = [pl.BlockSpec((x.shape[0] // 2, x.shape[1]), lambda i: (i, 0)) for x in out]
         out = pl.pallas_call(
             write,
-            grid=(4,),
+            grid=(2,),
             out_shape=[jax.ShapeDtypeStruct(x.shape, x.dtype) for x in out],
             in_specs=blocks,
             out_specs=blocks,

time: 63.9 us -> 61.3 us (0.959); the launches traced: 63.7 us -> 60.1 us
  Pallas kernels: 63.1 us -> 59.5 us
    pallas_call x1, Pallas kernels: 59.2 us -> 56.7 us  [body(): pl.pallas_call(functools.partial(kernel, sizes), out_shape=(jax.ShapeDtyp...]
    pallas_call x1, Pallas kernels: 3.84 us -> 2.77 us  [body(): pl.pallas_call(write, grid=(2,), out_shape=[jax.ShapeDtypeStruct(x.shape,...]
where the time goes in v4:
time: 61.3 us; the launch traced here: 60.1 us
  Pallas kernels  59.5 us (97%)
  between operations  0.64 us (1%)
    pallas_call x1, Pallas kernels, body(): pl.pallas_call(functools.partial(kernel, sizes), out_shape=(jax.ShapeDtyp...  56.7 us
    pallas_call x1, Pallas kernels, body(): pl.pallas_call(write, grid=(2,), out_shape=[jax.ShapeDtypeStruct(x.shape,...  2.77 us

profile of v4, /device:TPU:11, one launch (start us, length us, event | category | flops | bytes accessed | tf_op | source)
XLA Modules:
  0.0 60.1 jit_solution(15751501963909770814)
XLA Ops:
  0.6 56.7 %attention_backward.1 = (bf16[128,4096]{1,0:T(8,128)(2,1)}, bf16[128,4096]{1,0:T(8,128)(2,1)}, bf16[128,512]{1,0:T(8,128)(2,1)}, f32[128,512]{1,0:T(8,128)}) custom-call(bf16[128,4096]{1,0:T(8,128)(2,1)} %bitcast.7, bf16[128,4096]{1,0:T(8,128)(2,1)} %bitcast.8, bf16[128,512]{1,0:T(8,128)(2,1)} %bitcast.10, bf16[128,4096]{1,0:T(8,128)(2,1)} %bitcast.9, ...), custom_call_target="tpu_custom_call" | custom-call | tf_op jit(solution)/shard_map/attention_backward/pallas_call | solution.py:411
  57.3 2.8 %write.1 = (bf16[128,4096]{1,0:T(8,128)(2,1)}, bf16[128,4096]{1,0:T(8,128)(2,1)}, bf16[128,512]{1,0:T(8,128)(2,1)}, f32[128,512]{1,0:T(8,128)}) custom-call(bf16[128,4096]{1,0:T(8,128)(2,1)} %get-tuple-element.12.refs_0_, bf16[128,4096]{1,0:T(8,128)(2,1)} %get-tuple-element.13.refs_1_, bf16[128,512]{1,0:T(8,128)(2,1)} %get-tuple-element.14.refs_2_, ...), custom_call_target="tpu_custom_call" | custom-call | tf_op jit(solution)/shard_map/write/pallas_call | solution.py:467
